TPU v7x, 1024 devices: a whole 8x8x8 slice. The times are simulated.
1024 devices in a mesh: dp: 128 (over y, x, core), tensor: 8 (over z).
Axes of the slice: x: 8, y: 8, z: 8, core: 2. Of those that a mesh axis runs over, the one named last changes fastest.
Arguments:
- gradient: bfloat16 [128, 512, 512], P(None, 'dp', 'tensor')
- left_root: float32 [256, 512, 512], P('dp')
- right_root: float32 [256, 512, 512], P('dp')
- counts: int32 [128], replicated, may hold values from 0 to 2, as said below
- slot_table: int32 [128, 2], replicated, may hold values from 0 to 127
Outputs:
- update: bfloat16 [128, 512, 512], P(None, 'dp', 'tensor')
Inputs may be any that keep to these rules, and one draw needn't show every extreme that they name: Owner o holds the blocks slot_table[o, 0] to slot_table[o, counts[o] - 1]; over all owners every block is held exactly once; the other entries of slot_table are arbitrary block numbers.
All inputs are finite; a program needn't handle non-finite values.
Results may differ from a plain program's by a relative error of at most 0.001.
Values may be sent and summed in bfloat16 or wider, within the bound.
A program may use at most 32 MiB of HBM per device.

v0:
```python
import jax
import jax.numpy as jnp
from jax import lax
from jax.experimental import pallas as pl
from jax.experimental.pallas import tpu as pltpu
from jax.sharding import PartitionSpec as P

MESH = pl.DeviceIdType.MESH
EPSILON = 1e-06
BLK = 512
NB = 128
NY, NX, NXC, NZ = 8, 8, 16, 8
F32, BF16 = jnp.float32, jnp.bfloat16
PLANES = 4
FAR_FIRST = (4, 3, 5, 2, 6, 1, 7, 0)
BATCHES = ((0, 4), (4, 2), (6, 2))
EARLY_X = (0, 1, 2, 7, 3, 6, 5, 4)
EARLY_Y = (0, 1, 2, 3, 7, 6, 5, 4)


def iota(shape, dim):
    return lax.broadcasted_iota(jnp.int32, shape, dim)


def one_where(mask):
    return jnp.where(mask, 1.0, 0.0).astype(BF16)


def dot(a, b):
    return jnp.dot(a, b, preferred_element_type=F32)


def dot_nt(a, b):
    return lax.dot_general(a, b, (((1,), (1,)), ((), ())), preferred_element_type=F32)


def dot_tn(a, b):
    return lax.dot_general(a, b, (((0,), (0,)), ((), ())), preferred_element_type=F32)


def split(value):
    high = value.astype(BF16)
    return high, (value - high.astype(F32)).astype(BF16)


def kernel(
    grad, left, right, counts, table, out,
    grad_v, left_v, right_v, counts_v, table_v,
    send1, recv1, send2, recv2, send3, recv3, send4, recv4,
    left_high, left_low, right_high, right_low, ungroup, place, partial,
    local_sem, send_sem, recv_sem, piece_sem, panel_sem,
):
    dp, z = lax.axis_index("dp"), lax.axis_index("tensor")
    y, xc = dp // NXC, lax.rem(dp, NXC)
    x, core = xc // 2, lax.rem(xc, 2)
    slot = lax.rem(z // 2, 2)
    relays = z < PLANES
    handles = relays & (core == lax.rem(z, 2))

    fetch = [
        pltpu.make_async_copy(table, table_v, local_sem.at[0]),
        pltpu.make_async_copy(grad, grad_v, local_sem.at[1]),
        pltpu.make_async_copy(counts, counts_v, local_sem.at[2]),
    ]
    for copy in fetch:
        copy.start()
    fetch_left = pltpu.make_async_copy(left.at[slot], left_v, local_sem.at[3])
    fetch_right = pltpu.make_async_copy(right.at[slot], right_v, local_sem.at[4])

    barrier = pltpu.get_barrier_semaphore()

    @pl.when(relays)
    def _():
        for dy in FAR_FIRST:
            for dz in FAR_FIRST:
                if dy or dz:
                    peer = {"dp": lax.rem(y + dy, NY) * NXC + xc, "tensor": lax.rem(z + dz, NZ)}
                    pl.semaphore_signal(barrier, inc=1, device_id=peer, device_id_type=MESH)

    @pl.when(handles)
    def _():
        for step in range(1, NXC):
            peer = {"dp": y * NXC + lax.rem(xc + step, NXC)}
            pl.semaphore_signal(barrier, inc=1, device_id=peer, device_id_type=MESH)
        fetch_left.start()
        fetch_right.start()

    row, col = iota((256, 256), 0), iota((256, 256), 1)
    source = (row // 128) * 128 + ((row // 8) % 8) * 16 + (row % 8) * 2 + (row // 64) % 2
    order = one_where(col == source)
    block = iota((NB, NB), 0)
    fetch[0].wait()
    hit = [block == table_v[c : c + 1, :] for c in (0, 1)]
    pick = dot_nt(order, one_where(jnp.concatenate(hit, axis=1))).astype(BF16)
    fetch[1].wait()
    pieces = [dot_nt(pick, grad_v[128 * h : 128 * h + 128, :]).reshape(32, 8, 128) for h in (0, 1)]
    send1[...] = jnp.concatenate(pieces, axis=1).astype(BF16).reshape(PLANES, NY, 16, 128)

    def prepare():
        fetch[2].wait()
        row, col = iota((256, 256), 0), iota((256, 256), 1)
        order = one_where(col == (row % 2) * 128 + ((row // 2) % 8) * 16 + row // 16)
        live = [hit[c] & (counts_v[0:1, :] > c) for c in (0, 1)]
        place[...] = dot_nt(order, one_where(jnp.concatenate(live, axis=1))).astype(BF16)
        row, col = iota((BLK, BLK), 0), iota((BLK, BLK), 1)
        ungroup[...] = one_where(col == (row % 16) * 32 + (row // 32) * 2 + (row // 16) % 2)

    pl.when(relays)(prepare)

    @pl.when(handles)
    def _():
        row, col = iota((BLK, BLK), 0), iota((BLK, BLK), 1)
        rows = one_where(col == (row % 256) * 2 + row // 256)
        p = col % 256
        columns = one_where(row == ((p // 2) % 8) * 64 + (p // 16) * 4 + (p % 2) * 2 + col // 256)
        fetch_left.wait()
        high, low = split(left_v[...])
        left_high[...] = dot(dot(rows, high).astype(BF16), columns).astype(BF16)
        left_low[...] = dot(dot(rows, low).astype(BF16), columns).astype(BF16)
        fetch_right.wait()
        high, low = split(right_v[...])
        right_high[...] = high
        right_low[...] = low

    awaited = jnp.where(relays, PLANES * NY - 1 + jnp.where(handles, 7, 8), PLANES * NY)
    pl.semaphore_wait(barrier, awaited)

    def put(source, target, sent_on, lands_on, device):
        pltpu.make_async_remote_copy(
            src_ref=source,
            dst_ref=target,
            send_sem=sent_on,
            recv_sem=lands_on,
            device_id=device,
            device_id_type=MESH,
        ).start()

    def put_unless_here(here, source, target, sent_on, lands_on, device):
        @pl.when(jnp.logical_not(here))
        def _():
            put(source, target, sent_on, lands_on, device)

        @pl.when(here)
        def _():
            pltpu.make_async_copy(source, target, lands_on).start()

    def take(ref, sem):
        pltpu.make_async_copy(ref, ref, sem).wait()

    batch = jnp.where(z < 4, 0, z // 2 - 1)
    for dy in FAR_FIRST:
        there = lax.rem(y + dy, NY)
        for plane in (3, 2, 1, 0):
            source, target = send1.at[plane, there], recv1.at[z, y]
            device = {"dp": there * NXC + xc, "tensor": plane}
            if dy:
                put(source, target, send_sem.at[0], piece_sem.at[batch], device)
            else:
                put_unless_here(z == plane, source, target, send_sem.at[0], piece_sem.at[batch], device)

    pl.when(jnp.logical_not(relays))(prepare)

    @pl.when(relays)
    def _():
        row, col = iota((128, 128), 0), iota((128, 128), 1)
        turn = one_where(col == ((row // 2) % 8) * 16 + (row % 2) * 8 + row // 16)
        for batch, (start, size) in enumerate(BATCHES):
            planes = pl.ds(start, size)
            take(recv1.at[planes], piece_sem.at[batch])
            arrived = [recv1[t].reshape(128, 128) for t in range(start, start + size)]
            turned = dot(turn, jnp.concatenate(arrived, axis=1)).astype(BF16)
            for k in range(size):
                send2[start + k] = turned[:, 128 * k : 128 * k + 128].reshape(NX, 16, 128)
            lands_on = panel_sem.at[start // 4]
            for dx in FAR_FIRST:
                there = lax.rem(x + dx, NX)
                source, target = send2.at[planes, there], recv2.at[planes, xc]
                device = {"dp": y * NXC + there * 2 + lax.rem(z, 2)}
                if dx:
                    put(source, target, send_sem.at[1], lands_on, device)
                else:
                    put_unless_here(handles, source, target, send_sem.at[1], lands_on, device)

    @pl.when(handles)
    def _():
        def half(u):
            take(recv2.at[pl.ds(4 * u, 4)], panel_sem.at[u])
            panels = [recv2[t].reshape(256, 128) for t in range(4 * u, 4 * u + 4)]
            even = jnp.concatenate([panel[:, :64] for panel in panels], axis=1)
            odd = jnp.concatenate([panel[:, 64:] for panel in panels], axis=1)
            held = jnp.concatenate([even, odd], axis=0)
            high, low = split(dot(left_high[...], held) + dot(left_low[...], held))
            first, second = right_high[256 * u : 256 * u + 256, :], right_low[256 * u : 256 * u + 256, :]
            wide = held.astype(F32)
            return dot(high, first) + dot(low, first) + dot(high, second), jnp.sum(wide * wide, keepdims=True)

        partial[...], first_sum = half(0)
        rest, second_sum = half(1)
        direction = partial[...] + rest
        entries = BLK * BLK
        grad_mean = (first_sum + second_sum) / entries
        dir_mean = jnp.sum(direction * direction, keepdims=True) / entries
        factor = jnp.sqrt(grad_mean) * lax.rsqrt(dir_mean + EPSILON)
        mine = (iota((1, NB), 1) == dp) & (counts_v[...] > slot)
        alive = jnp.max(jnp.where(mine, 1.0, 0.0), keepdims=True) > 0.0
        for t in range(0, NZ, 2):
            update = jnp.where(alive, direction[:, 64 * t : 64 * t + 128] * factor, 0.0).astype(BF16)
            upper, lower = update[:256], update[256:]
            first = jnp.concatenate([upper[:, :64], lower[:, :64]], axis=1)
            second = jnp.concatenate([upper[:, 64:], lower[:, 64:]], axis=1)
            send3[:, t] = first.reshape(NY, 32, 128)
            send3[:, t + 1] = second.reshape(NY, 32, 128)
            for plane in (t, t + 1):
                for there in EARLY_Y:
                    source, target = send3.at[there, plane], recv3.at[y * 2 + slot]
                    device = {"dp": there * NXC + xc, "tensor": plane}
                    if plane < PLANES:
                        here = (there == y) & (plane == z)
                        put_unless_here(here, source, target, send_sem.at[2], recv_sem.at[0], device)
                    else:
                        put(source, target, send_sem.at[2], recv_sem.at[0], device)

    take(recv3, recv_sem.at[0])
    grouped = dot(ungroup[...], recv3[...].reshape(BLK, 128)).astype(BF16)
    send4[...] = grouped.reshape(NXC, 32, 128)
    for there_x in EARLY_X:
        for there in (there_x * 2 + 1, there_x * 2):
            device = {"dp": y * NXC + there}
            put_unless_here(there == xc, send4.at[there], recv4.at[xc], send_sem.at[3], recv_sem.at[1], device)

    take(recv4, recv_sem.at[1])
    for h in (0, 1):
        returned = recv4[:, 16 * h : 16 * h + 16, :].reshape(256, 128)
        out[128 * h : 128 * h + 128, :] = dot_tn(returned, place[...]).astype(BF16)

    take(send4.at[pl.ds(0, 15)], send_sem.at[3])

    @pl.when(relays)
    def _():
        take(send1.at[pl.ds(0, 3)], send_sem.at[0])
        take(send1.at[3, pl.ds(0, 7)], send_sem.at[0])
        take(send2.at[:, pl.ds(0, 7)], send_sem.at[1])

    @pl.when(jnp.logical_not(relays))
    def _():
        take(send1, send_sem.at[0])

    @pl.when(relays & jnp.logical_not(handles))
    def _():
        take(send2.at[:, 7], send_sem.at[1])

    @pl.when(handles)
    def _():
        take(send3.at[pl.ds(0, 7)], send_sem.at[2])
        take(send3.at[7, pl.ds(0, 7)], send_sem.at[2])


def body(gradient, left_root, right_root, counts, slot_table):
    pieces = jnp.transpose(gradient, (1, 2, 0)).reshape(256, NB)
    operands = (pieces, left_root, right_root, counts.reshape(1, NB), slot_table.T)
    operands = [pltpu.with_memory_space_constraint(operand, pltpu.HBM) for operand in operands]
    vmem = pltpu.VMEM
    message = (32, 128)
    update = pl.pallas_call(
        kernel,
        out_shape=jax.ShapeDtypeStruct((256, NB), BF16),
        in_specs=[pl.BlockSpec(memory_space=pltpu.HBM)] * 5,
        out_specs=pl.BlockSpec(memory_space=pltpu.VMEM),
        scratch_shapes=[
            vmem((256, NB), BF16),
            vmem((BLK, BLK), F32),
            vmem((BLK, BLK), F32),
            vmem((1, NB), jnp.int32),
            vmem((2, NB), jnp.int32),
            vmem((PLANES, NY, 16, 128), BF16),
            vmem((NZ, NY, 16, 128), BF16),
            vmem((NZ, NX, 16, 128), BF16),
            vmem((NZ, NXC, 16, 128), BF16),
            vmem((NY, NZ, *message), BF16),
            vmem((16, *message), BF16),
            vmem((16, *message), BF16),
            vmem((16, *message), BF16),
            vmem((BLK, BLK), BF16),
            vmem((BLK, BLK), BF16),
            vmem((BLK, BLK), BF16),
            vmem((BLK, BLK), BF16),
            vmem((BLK, BLK), BF16),
            vmem((256, NB), BF16),
            vmem((BLK, BLK), F32),
            pltpu.SemaphoreType.DMA((5,)),
            pltpu.SemaphoreType.DMA((4,)),
            pltpu.SemaphoreType.DMA((2,)),
            pltpu.SemaphoreType.DMA((3,)),
            pltpu.SemaphoreType.DMA((2,)),
        ],
        compiler_params=pltpu.CompilerParams(
            collective_id=0, has_side_effects=True, vmem_limit_bytes=40 * 1024 * 1024
        ),
    )(*operands)
    return jnp.transpose(update.reshape(4, 64, NB), (2, 0, 1))


def solution(mesh):
    return jax.shard_map(
        body,
        mesh=mesh,
        in_specs=(P(None, "dp", "tensor"), P("dp", None, None), P("dp", None, None), P(), P()),
        out_specs=P(None, "dp", "tensor"),
        check_vma=False,
    )
```

profile of v0, /device:TPU:1, one launch (start us, length us, event | category | flops | bytes accessed | tf_op | source)
XLA Modules:
  0.0 46.4 jit_solution(3396422682969144515)
XLA Ops:
  0.0 45.8 %shard_map.55 = bf16[256,128]{1,0:T(8,128)(2,1)S(1)} custom-call(bf16[256,128]{1,0:T(8,128)(2,1)} %bitcast.9, f32[2,512,512]{2,1,0:T(8,128)} %left.1, f32[2,512,512]{2,1,0:T(8,128)} %right.1, s32[1,128]{1,0:T(1,128)} %bitcast.11, s32[2,128]{1,0:T(2,128)} %bitcast.10), custom_call_target="tpu_custom_call" | custom-call | tf_op jit(solution)/shard_map/pallas_call | solution.py:264
  45.8 0.6 %copy.7 = bf16[128,4,64]{0,2,1:T(8,128)(2,1)} copy(bf16[128,4,64]{0,2,1:T(8,128)(2,1)S(1)} %bitcast.8) | data formatting | bytes 131072
where the time goes:
time: 46.6 us; the launch traced here: 46.4 us
  Pallas kernels  45.8 us (98%)
  local copies, waits for them, and re-layouts  0.63 us (1%)
    pallas_call x1, Pallas kernels, body(): pl.pallas_call(kernel, out_shape=jax.ShapeDtypeStruct((256, NB), BF16), i...  45.8 us

commit v1 on v0

--- a/solution.py
+++ b/solution.py
@@ -24,6 +24,10 @@
 
 def one_where(mask):
     return jnp.where(mask, 1.0, 0.0).astype(BF16)
+
+
+def reorder(n, place_of):
+    return one_where(iota((n, n), 0) == place_of(iota((1, n), 1)))
 
 
 def dot(a, b):
@@ -85,9 +89,7 @@
         fetch_left.start()
         fetch_right.start()
 
-    row, col = iota((256, 256), 0), iota((256, 256), 1)
-    source = (row // 128) * 128 + ((row // 8) % 8) * 16 + (row % 8) * 2 + (row // 64) % 2
-    order = one_where(col == source)
+    order = reorder(256, lambda k: (k & 128) + ((k & 1) << 6) + (((k >> 4) & 7) << 3) + ((k >> 1) & 7))
     block = iota((NB, NB), 0)
     fetch[0].wait()
     hit = [block == table_v[c : c + 1, :] for c in (0, 1)]
@@ -98,21 +100,17 @@
 
     def prepare():
         fetch[2].wait()
-        row, col = iota((256, 256), 0), iota((256, 256), 1)
-        order = one_where(col == (row % 2) * 128 + ((row // 2) % 8) * 16 + row // 16)
+        by_owner = reorder(256, lambda k: ((k & 15) << 4) + (((k >> 4) & 7) << 1) + (k >> 7))
         live = [hit[c] & (counts_v[0:1, :] > c) for c in (0, 1)]
-        place[...] = dot_nt(order, one_where(jnp.concatenate(live, axis=1))).astype(BF16)
-        row, col = iota((BLK, BLK), 0), iota((BLK, BLK), 1)
-        ungroup[...] = one_where(col == (row % 16) * 32 + (row // 32) * 2 + (row // 16) % 2)
+        place[...] = dot_nt(by_owner, one_where(jnp.concatenate(live, axis=1))).astype(BF16)
+        ungroup[...] = reorder(BLK, lambda k: (((k >> 1) & 15) << 5) + ((k & 1) << 4) + (k >> 5))
 
     pl.when(relays)(prepare)
 
     @pl.when(handles)
     def _():
-        row, col = iota((BLK, BLK), 0), iota((BLK, BLK), 1)
-        rows = one_where(col == (row % 256) * 2 + row // 256)
-        p = col % 256
-        columns = one_where(row == ((p // 2) % 8) * 64 + (p // 16) * 4 + (p % 2) * 2 + col // 256)
+        rows = reorder(BLK, lambda k: ((k & 1) << 8) + (k >> 1))
+        columns = reorder(BLK, lambda k: (((k >> 1) & 7) << 6) + (((k >> 4) & 15) << 2) + ((k & 1) << 1) + (k >> 8))
         fetch_left.wait()
         high, low = split(left_v[...])
         left_high[...] = dot(dot(rows, high).astype(BF16), columns).astype(BF16)
@@ -135,14 +133,13 @@
             device_id_type=MESH,
         ).start()
 
-    def put_unless_here(here, source, target, sent_on, lands_on, device):
+    def put_unless_here(here, *args):
         @pl.when(jnp.logical_not(here))
         def _():
-            put(source, target, sent_on, lands_on, device)
-
-        @pl.when(here)
-        def _():
-            pltpu.make_async_copy(source, target, lands_on).start()
+            put(*args)
+
+    def put_here(source, target, lands_on):
+        pltpu.make_async_copy(source, target, lands_on).start()
 
     def take(ref, sem):
         pltpu.make_async_copy(ref, ref, sem).wait()
@@ -162,8 +159,8 @@
 
     @pl.when(relays)
     def _():
-        row, col = iota((128, 128), 0), iota((128, 128), 1)
-        turn = one_where(col == ((row // 2) % 8) * 16 + (row % 2) * 8 + row // 16)
+        put_here(send1.at[lax.rem(z, PLANES), y], recv1.at[z, y], piece_sem.at[0])
+        turn = reorder(128, lambda k: ((k & 7) << 4) + ((k >> 4) << 1) + ((k >> 3) & 1))
         for batch, (start, size) in enumerate(BATCHES):
             planes = pl.ds(start, size)
             take(recv1.at[planes], piece_sem.at[batch])
@@ -180,6 +177,10 @@
                     put(source, target, send_sem.at[1], lands_on, device)
                 else:
                     put_unless_here(handles, source, target, send_sem.at[1], lands_on, device)
+
+                    @pl.when(handles)
+                    def _(source=source, target=target, lands_on=lands_on):
+                        put_here(source, target, lands_on)
 
     @pl.when(handles)
     def _():
@@ -219,6 +220,11 @@
                         put_unless_here(here, source, target, send_sem.at[2], recv_sem.at[0], device)
                     else:
                         put(source, target, send_sem.at[2], recv_sem.at[0], device)
+            if t < PLANES:
+
+                @pl.when(slot == t // 2)
+                def _():
+                    put_here(send3.at[y, lax.rem(z, PLANES)], recv3.at[y * 2 + slot], recv_sem.at[0])
 
     take(recv3, recv_sem.at[0])
     grouped = dot(ungroup[...], recv3[...].reshape(BLK, 128)).astype(BF16)
@@ -227,6 +233,7 @@
         for there in (there_x * 2 + 1, there_x * 2):
             device = {"dp": y * NXC + there}
             put_unless_here(there == xc, send4.at[there], recv4.at[xc], send_sem.at[3], recv_sem.at[1], device)
+    put_here(send4.at[xc], recv4.at[xc], recv_sem.at[1])
 
     take(recv4, recv_sem.at[1])
     for h in (0, 1):

time: 46.6 us -> 46.9 us (level)
  no operation moved by 1% of the time
where the time goes in v1:
time: 46.9 us; the launch traced here: 46.7 us
  Pallas kernels  46.1 us (98%)
  local copies, waits for them, and re-layouts  0.63 us (1%)
    pallas_call x1, Pallas kernels, body(): pl.pallas_call(kernel, out_shape=jax.ShapeDtypeStruct((256, NB), BF16), i...  46.1 us

profile of v1, /device:TPU:1, one launch (start us, length us, event | category | flops | bytes accessed | tf_op | source)
XLA Modules:
  0.0 46.7 jit_solution(14099782295944158758)
XLA Ops:
  0.0 46.1 %shard_map.55 = bf16[256,128]{1,0:T(8,128)(2,1)S(1)} custom-call(bf16[256,128]{1,0:T(8,128)(2,1)} %bitcast.9, f32[2,512,512]{2,1,0:T(8,128)} %left.1, f32[2,512,512]{2,1,0:T(8,128)} %right.1, s32[1,128]{1,0:T(1,128)} %bitcast.11, s32[2,128]{1,0:T(2,128)} %bitcast.10), custom_call_target="tpu_custom_call" | custom-call | tf_op jit(solution)/shard_map/pallas_call | solution.py:271
  46.1 0.6 %copy.7 = bf16[128,4,64]{0,2,1:T(8,128)(2,1)} copy(bf16[128,4,64]{0,2,1:T(8,128)(2,1)S(1)} %bitcast.8) | data formatting | bytes 131072
